TPU v7x, 256 devices: a whole 4x4x8 slice. The times are simulated.
256 devices in a mesh: lag: 8 (over x, z_hi), space: 32 (over z_lo, y, core).
Axes of the slice: x: 4, y: 4, z: 8 (z_hi: 2, z_lo: 4; z = z_hi * 4 + z_lo), core: 2. Of those that a mesh axis runs over, the one named last changes fastest.
Arguments:
- lagged: bfloat16 [8, 5120, 136, 128], P('lag', 'space')
- weights: float32 [2048, 128, 128], P(('space', 'lag'))
- cell_index: int32 [5120], P('space'), may hold values from 0 to 64, as said below
- fraction: float32 [5120], P('space'), may hold values from 0.05 to 0.95
Outputs:
- smoothed: bfloat16 [8, 5120, 136, 128], P('lag', 'space')
Inputs may be any that keep to these rules, and one draw needn't show every extreme that they name: `cell_index`: within each block of 160 columns of one index of space, the first column has cell 0 and the second cell 64.
All inputs are finite; a program needn't handle non-finite values.
Results may differ from a plain program's by a relative error of at most 0.0057.
Values may be sent and summed in bfloat16 or wider, within the bound.
No kernel may reach another device: no remote copies, remote signals or barrier semaphores. Data moves between devices by JAX's collectives and lax.ppermute only.
A program may use at most 128 MiB of HBM per device.

v0:
```python
import jax
import jax.numpy as jnp
from jax import lax
from jax.sharding import PartitionSpec as P


def with_halo(cells, sides, width):
    for axis, dim in sides:
        count = lax.axis_size(axis)
        head = lax.slice_in_dim(cells, 0, width, axis=dim)
        tail = lax.slice_in_dim(cells, cells.shape[dim] - width, cells.shape[dim], axis=dim)
        cells = jnp.concatenate(
            [
                lax.ppermute(tail, axis, [(i, (i + 1) % count) for i in range(count)]),
                cells,
                lax.ppermute(head, axis, [((i + 1) % count, i) for i in range(count)]),
            ],
            axis=dim,
        )
    return cells


def shards(lagged, weights, cell_index, fraction):
    spatial_block = lax.all_gather(weights, "lag", axis=0, tiled=True)
    extended = with_halo(spatial_block, (("space", 0),), 1)
    states = lagged[0]
    center = jnp.mean(states, axis=-1, keepdims=True, dtype=jnp.float32)
    anomaly_spread = (states.astype(jnp.float32) - center).astype(jnp.bfloat16)
    left_weight = jnp.take(extended, cell_index, axis=0)
    right_weight = jnp.take(extended, cell_index + 1, axis=0)
    scaled = fraction[:, None, None]
    shifted_columns = jnp.einsum(
        "pan,pnt->pat",
        anomaly_spread,
        ((1.0 - scaled) * left_weight + scaled * right_weight).astype(jnp.bfloat16),
        preferred_element_type=jnp.float32,
    )
    smoothed = (center + shifted_columns).astype(jnp.bfloat16)
    return smoothed[None]


def solution(mesh):
    in_specs = (
        P("lag", "space", None, None),
        P(("space", "lag"), None, None),
        P("space"),
        P("space"),
    )
    out_specs = P("lag", "space", None, None)
    return jax.shard_map(shards, mesh=mesh, in_specs=in_specs, out_specs=out_specs, check_vma=False)
```

profile of v0, /device:TPU:32, one launch (start us, length us, event | category | flops | bytes accessed | tf_op | source)
XLA Modules:
  0.0 177.3 jit_solution(15041560041834414959)
XLA Ops:
  6.5 0.0 all-gather.2.cloned.1.call-start
  6.5 0.7 all-gather.2.cloned.1.call-update
  7.3 0.7 broadcast_subtract_fusion
  7.9 0.7 compare_and_fusion.1
  8.6 0.7 compare_select_fusion.1
  9.3 5.4 %convert_reduce_fusion = f32[160,136]{1,0:T(8,128)S(1)} fusion(bf16[1,160,136,128]{3,2,1,0:T(8,128)(2,1)} %param.6), kind=kLoop, calls=%fused_computation.3 | loop fusion | flops 5548800 | bytes 5657600 | tf_op jit(solution)/shard_map/reduce_sum | solution.py:27
  14.7 103.9 %all-gather.2.cloned.1.call-done = f32[64,128,128]{2,1,0:T(8,128)} async-done(((f32[8,128,128]{2,1,0:T(8,128)}), f32[64,128,128]{2,1,0:T(8,128)}) %all-gather.2.cloned.1.call-update) | async-done | bytes 4194320 | tf_op jit(solution)/shard_map/all_gather | solution.py:24
  118.6 0.9 fusion.19
  119.5 0.1 collective-permute-start
  119.6 3.8 %collective-permute-start.1 = (f32[1,128,128]{2,1,0:T(8,128)S(1)}, f32[1,128,128]{2,1,0:T(8,128)S(1)}, u32[]{:S(2)}, u32[]{:S(2)}) collective-permute-start(f32[1,128,128]{2,1,0:T(8,128)S(1)} %get-tuple-element.6), channel_id=1, source_target_pairs={{1,0},{2,1},{3,2},{4,3},{5,4},{6,5},{7,6},{8,7},{9,8},{10,9},{11,1... | collective-permute-start | bytes 196616 | tf_op jit(solution)/shard_map/ppermute | solution.py:16
  123.5 1.9 %collective-permute-done = f32[1,128,128]{2,1,0:T(8,128)S(1)} collective-permute-done((f32[1,128,128]{2,1,0:T(8,128)S(1)}, f32[1,128,128]{2,1,0:T(8,128)S(1)}, u32[]{:S(2)}, u32[]{:S(2)}) %collective-permute-start) | collective-permute-done | bytes 65568 | tf_op jit(solution)/shard_map/ppermute | solution.py:14
  125.4 0.6 constant_dynamic-update-slice_fusion.2
  126.0 4.7 %constant_dynamic-update-slice_fusion.1 = f32[66,128,128]{2,1,0:T(8,128)} fusion(f32[66,128,128]{2,1,0:T(8,128)} %constant_dynamic-update-slice_fusion.2, f32[64,128,128]{2,1,0:T(8,128)} %all-gather.2.cloned.1.call-done), kind=kLoop, calls=%fused_computation.21 | loop fusion | bytes 8388608
  130.7 0.0 collective-permute-done.1
  130.7 0.6 constant_dynamic-update-slice_fusion
  131.4 12.4 %gather_fusion.1 = f32[160,128,128]{2,1,0:T(8,128)} fusion(f32[66,128,128]{2,1,0:T(8,128)} %constant_dynamic-update-slice_fusion, s32[1024]{0:T(1024)S(1)} %get-tuple-element.12), kind=kCustom, calls=%fused_computation.1.clone | custom fusion | bytes 20972160 | tf_op jit(solution)/shard_map/jit(_take)/gather | solution.py:30
  143.7 0.0 copy-start
  143.7 12.2 %gather_fusion = f32[160,128,128]{2,1,0:T(8,128)} fusion(f32[66,128,128]{2,1,0:T(8,128)} %constant_dynamic-update-slice_fusion, s32[1024]{0:T(1024)S(1)} %get-tuple-element.13), kind=kCustom, calls=%fused_computation.clone | custom fusion | bytes 20972160 | tf_op jit(solution)/shard_map/jit(_take)/gather | solution.py:29
  156.0 0.0 copy-done
  156.0 14.5 %fusion.4 = bf16[1,160,136,128]{3,2,1,0:T(8,128)(2,1)} fusion(f32[160,136]{1,0:T(8,128)S(1)} %broadcast_multiply_fusion, f32[160,128,128]{2,1,0:T(8,128)} %gather_fusion.1, f32[160,128,128]{2,1,0:T(8,128)} %gather_fusion, f32[160]{0:T(256)S(1)} %copy-done, f32[160]{0:T(256)S(1)} %broadcast_subtract_fusion, pred[160]{0:T(512)(128)(4,1)S(1)} %get-tuple-element.9, ...), kind=kOutput, calls=%fused_computation.11 | convolution fusion | flops 742686720 | bytes 32201280 | tf_op jit(solution)/shard_map/pan,pnt->pat/dot_general | solution.py:32
  (2 shorter events, 0.0 us)
Async XLA Ops:
  6.5 112.1 %all-gather.2.cloned.1.call-start = ((), (), s32[]{:S(2)}) async-start(), calls=%async_computation | async-start | bytes 4718592 | tf_op jit(solution)/shard_map/all_gather | solution.py:24
  119.5 5.9 %collective-permute-start = (f32[1,128,128]{2,1,0:T(8,128)S(1)}, f32[1,128,128]{2,1,0:T(8,128)S(1)}, u32[]{:S(2)}, u32[]{:S(2)}) collective-permute-start(f32[1,128,128]{2,1,0:T(8,128)S(1)} %get-tuple-element.7), channel_id=1, source_target_pairs={{0,1},{1,2},{2,3},{3,4},{4,5},{5,6},{6,7},{7,8},{8,9},{9,10},{10,1... | collective-permute-start | bytes 196616 | tf_op jit(solution)/shard_map/ppermute | solution.py:14
  119.6 11.1 %collective-permute-start.1 = (f32[1,128,128]{2,1,0:T(8,128)S(1)}, f32[1,128,128]{2,1,0:T(8,128)S(1)}, u32[]{:S(2)}, u32[]{:S(2)}) collective-permute-start(f32[1,128,128]{2,1,0:T(8,128)S(1)} %get-tuple-element.6), channel_id=1, source_target_pairs={{1,0},{2,1},{3,2},{4,3},{5,4},{6,5},{7,6},{8,7},{9,8},{10,9},{11,1... | collective-permute-start | bytes 196616 | tf_op jit(solution)/shard_map/ppermute | solution.py:16
  143.7 12.3 %copy-start = (f32[160]{0:T(256)S(1)}, f32[160]{0:T(256)}, u32[]{:S(2)}) copy-start(f32[160]{0:T(256)} %param.9) | copy-start | bytes 1924
Sparse Core Ops, SparseCore 0:
  10.0 108.6 all-gather.1
where the time goes:
time: 180 us; the launch traced here: 177 us
  waiting for transfers between devices  107 us (59%)
  local copies, waits for them, and re-layouts  31.5 us (18%)
  matrix products  14.5 us (8%)
  between operations  13.4 us (7%)
  other arithmetic  7.44 us (4%)
  starting transfers between devices  3.92 us (2%)
    all_gather x1, waiting for transfers between devices, shards(): spatial_block = lax.all_gather(weights, 'lag', axis=0, tiled=True)  104 us
    dot_general x1, matrix products, shards(): jnp.einsum('pan,pnt->pat', anomaly_spread, ((1.0 - scaled) * left_weight...  14.5 us
    gather x1, local copies, waits for them, and re-layouts, shards(): right_weight = jnp.take(extended, cell_index + 1, axis=0)  12.4 us
    gather x1, local copies, waits for them, and re-layouts, shards(): left_weight = jnp.take(extended, cell_index, axis=0)  12.2 us
    reduce_sum x1, other arithmetic, shards(): center = jnp.mean(states, axis=-1, keepdims=True, dtype=jnp.float32)  5.37 us
    unnamed x4, local copies, waits for them, and re-layouts  5.34 us
    ppermute x1, starting transfers between devices, with_halo(): lax.ppermute(head, axis, [((i + 1) % count, i) for i in range(count)])  3.83 us
  transfers between devices with their start and end apart: 3, of which 2 were waited for; matrix products, arithmetic and copies ran while one was open for 7% of the time, Pallas kernels for 0%

commit v1 on v0

v1 whole, which is shorter than its diff:
```python
import jax
import jax.numpy as jnp
from jax import lax
from jax.experimental import pallas as pl
from jax.experimental.pallas import tpu as pltpu
from jax.sharding import PartitionSpec as P

AXES = ("lag", "space")
BLOCK = 32


def send(block, step_x, step_z, step_space=0):
    lags, spaces = lax.axis_size("lag"), lax.axis_size("space")
    rows = lags // 2
    pairs = []
    for lag in range(lags):
        x, half = divmod(lag, 2)
        to = (x + step_x) % rows * 2 + (half + step_z) % 2
        shift = step_space[half] if step_space else 0
        pairs += [(lag * spaces + s, to * spaces + (s + shift) % spaces) for s in range(spaces)]
    return lax.ppermute(block, AXES, pairs)


def apply_kernel(me, cell, fraction, states_ref, *rest):
    parts, (left_ref, right_ref, out_ref, points) = rest[:8], rest[8:]
    size = parts[0].shape[0]
    step = pl.program_id(0)

    @pl.when(step == 0)
    def _():
        x, half = me[0] // 2, me[0] % 2
        for k, part in enumerate(parts):
            source = lax.rem(x + 4 - k % 4, 4) * 2 + lax.rem(half + k // 4, 2)
            points[pl.ds(1 + source * size, size)] = part[...]
        points[0] = left_ref[0]
        points[1 + 8 * size] = right_ref[0]

    def column(j, _):
        n = step * BLOCK + j
        c, f = cell[n], fraction[n]
        states = states_ref[j].astype(jnp.float32)
        center = jnp.mean(states, axis=-1, keepdims=True)
        spread = (states - center).astype(jnp.bfloat16)
        both = jnp.concatenate([points[c], points[c + 1]], axis=1)
        moved = jnp.dot(spread, both, preferred_element_type=jnp.float32)
        width = moved.shape[1] // 2
        out = center + (1.0 - f) * moved[:, :width] + f * moved[:, width:]
        out_ref[j] = out.astype(jnp.bfloat16)
        return 0

    lax.fori_loop(0, BLOCK, column, 0, unroll=True)


def shards(lagged, weights, cell_index, fraction):
    states = lagged[0]
    own = weights.astype(jnp.bfloat16)
    me = lax.axis_index("lag")
    x, half = me // 2, me % 2

    def along_x(block):
        return [block] + [send(block, k, 0) for k in (1, 2, 3)]

    across = send(own, 0, 1)
    same = along_x(own)
    other = along_x(across)
    held = jnp.where(half == 0, x, (x + 1) % 4)
    edges = [jnp.where(half == 0, p[:1], p[-1:]) for p in same]
    edge = jnp.where(held < 2, jnp.where(held == 0, edges[0], edges[1]), jnp.where(held == 2, edges[2], edges[3]))
    near = send(edge, 0, 0, (-1, 1))
    far = send(edge, 0, 1, (-1, 1))
    left = jnp.where(half == 0, far, near)
    right = jnp.where(half == 0, near, far)

    count, levels, members = states.shape
    block = pl.BlockSpec((BLOCK, levels, members), lambda i, *_: (i, 0, 0))
    whole = pl.BlockSpec(memory_space=pltpu.VMEM)
    points = 8 * own.shape[0] + 2
    smoothed = pl.pallas_call(
        apply_kernel,
        grid_spec=pltpu.PrefetchScalarGridSpec(
            num_scalar_prefetch=3,
            grid=(count // BLOCK,),
            in_specs=[block] + [whole] * 10,
            out_specs=block,
            scratch_shapes=[pltpu.VMEM((points, members, members), jnp.bfloat16)],
        ),
        out_shape=jax.ShapeDtypeStruct(states.shape, jnp.bfloat16),
        compiler_params=pltpu.CompilerParams(vmem_limit_bytes=24 << 20),
        cost_estimate=pl.CostEstimate(
            flops=4 * count * levels * members * members,
            bytes_accessed=4 * states.size,
            transcendentals=0,
        ),
    )(me.reshape(1), cell_index, fraction, states, *same, *other, left, right)
    return smoothed[None]


def solution(mesh):
    in_specs = (
        P("lag", "space", None, None),
        P(("space", "lag"), None, None),
        P("space"),
        P("space"),
    )
    out_specs = P("lag", "space", None, None)
    return jax.shard_map(shards, mesh=mesh, in_specs=in_specs, out_specs=out_specs, check_vma=False)
```

time: 180 us -> 49.3 us (0.27); the launches traced: 177 us -> 49.1 us
  waiting for transfers between devices: 107 us -> 14.9 us
  local copies, waits for them, and re-layouts: 31.5 us -> 3.93 us
  starting transfers between devices: 3.92 us -> 22.4 us
  matrix products: 14.5 us -> 0 us
  between operations: 13.4 us -> 0.06 us
  Pallas kernels: 0 us -> 6.64 us
  other arithmetic: 7.44 us -> 1.1 us
    all_gather x1 -> x0, waiting for transfers between devices: 104 us -> none  [shards(): spatial_block = lax.all_gather(weights, 'lag', axis=0, tiled=True)]
    gather x2 -> x0, local copies, waits for them, and re-layouts: 24.6 us -> none  [the longest x1 12.4 us: shards(): right_weight = jnp.take(extended, cell_index + 1, axis=0)]
    ppermute x2 -> x9, starting transfers between devices: 3.92 us -> 22.4 us  [send(): return lax.ppermute(block, AXES, pairs)]
    dot_general x1 -> x0, matrix products: 14.5 us -> none  [shards(): jnp.einsum('pan,pnt->pat', anomaly_spread, ((1.0 - scaled) * left_weight...]
    ppermute x2 -> x9, waiting for transfers between devices: 1.94 us -> 14.9 us  [send(): return lax.ppermute(block, AXES, pairs)]
    pallas_call x0 -> x1, Pallas kernels: none -> 6.64 us  [shards(): pl.pallas_call(apply_kernel, grid_spec=pltpu.PrefetchScalarGridSpec(num_s...]
    reduce_sum x1 -> x0, other arithmetic: 5.37 us -> none  [shards(): center = jnp.mean(states, axis=-1, keepdims=True, dtype=jnp.float32)]
    unnamed x4 -> x6, local copies, waits for them, and re-layouts: 5.34 us -> 3.93 us
  transfers between devices with their start and end apart: 3 -> 9, of which waited for: 2 -> 3; matrix products, arithmetic and copies ran while one was open for 7% -> 0% of each run, Pallas kernels for 0% -> 0%
where the time goes in v1:
time: 49.3 us; the launch traced here: 49.1 us
  starting transfers between devices  22.4 us (45%)
  waiting for transfers between devices  14.9 us (30%)
  Pallas kernels  6.64 us (13%)
  local copies, waits for them, and re-layouts  3.93 us (8%)
  other arithmetic  1.1 us (2%)
    ppermute x9, starting transfers between devices, send(): return lax.ppermute(block, AXES, pairs)  22.4 us
    ppermute x9, waiting for transfers between devices, send(): return lax.ppermute(block, AXES, pairs)  14.9 us
    pallas_call x1, Pallas kernels, shards(): pl.pallas_call(apply_kernel, grid_spec=pltpu.PrefetchScalarGridSpec(num_s...  6.64 us
    unnamed x6, local copies, waits for them, and re-layouts  3.93 us
    convert_element_type x1, other arithmetic, shards(): own = weights.astype(jnp.bfloat16)  1.08 us
  transfers between devices with their start and end apart: 9, of which 3 were waited for; matrix products, arithmetic and copies ran while one was open for 0% of the time, Pallas kernels for 0%

profile of v1, /device:TPU:32, one launch (start us, length us, event | category | flops | bytes accessed | tf_op | source)
XLA Modules:
  0.0 49.1 jit_solution(5851858407930880581)
XLA Ops:
  0.0 1.1 %convert_element_type.3.rest_0_ = bf16[8,128,128]{2,1,0:T(8,128)(2,1)S(1)} convert(f32[8,128,128]{2,1,0:T(8,128)} %param.5) | non-fusion elementwise | flops 131072 | bytes 786432 | tf_op jit(solution)/shard_map/convert_element_type | solution.py:56
  1.1 6.4 %collective-permute-start.3 = (bf16[8,128,128]{2,1,0:T(8,128)(2,1)S(1)}, bf16[8,128,128]{2,1,0:T(8,128)(2,1)S(1)}, u32[]{:S(2)}, u32[]{:S(2)}) collective-permute-start(bf16[8,128,128]{2,1,0:T(8,128)(2,1)S(1)} %convert_element_type.3.rest_0_), channel_id=1, source_target_pairs={{0,32},{1,33},{2,34},{3,35},{4,36},{5,37},{6,38},{7,39},{8,40},{9,... | collective-permute-start | bytes 786440 | tf_op jit(solution)/shard_map/ppermute | solution.py:21
  7.5 2.8 %collective-permute-start.2 = (bf16[8,128,128]{2,1,0:T(8,128)(2,1)S(1)}, bf16[8,128,128]{2,1,0:T(8,128)(2,1)S(1)}, u32[]{:S(2)}, u32[]{:S(2)}) collective-permute-start(bf16[8,128,128]{2,1,0:T(8,128)(2,1)S(1)} %convert_element_type.3.rest_0_), channel_id=1, source_target_pairs={{0,192},{1,193},{2,194},{3,195},{4,196},{5,197},{6,198},{7,199},{8... | collective-permute-start | bytes 786440 | tf_op jit(solution)/shard_map/ppermute | solution.py:21
  10.2 0.8 %collective-permute-start.1 = (bf16[8,128,128]{2,1,0:T(8,128)(2,1)S(1)}, bf16[8,128,128]{2,1,0:T(8,128)(2,1)S(1)}, u32[]{:S(2)}, u32[]{:S(2)}) collective-permute-start(bf16[8,128,128]{2,1,0:T(8,128)(2,1)S(1)} %convert_element_type.3.rest_0_), channel_id=1, source_target_pairs={{0,128},{1,129},{2,130},{3,131},{4,132},{5,133},{6,134},{7,135},{8... | collective-permute-start | bytes 786440 | tf_op jit(solution)/shard_map/ppermute | solution.py:21
  11.0 0.9 %collective-permute-start = (bf16[8,128,128]{2,1,0:T(8,128)(2,1)S(1)}, bf16[8,128,128]{2,1,0:T(8,128)(2,1)S(1)}, u32[]{:S(2)}, u32[]{:S(2)}) collective-permute-start(bf16[8,128,128]{2,1,0:T(8,128)(2,1)S(1)} %convert_element_type.3.rest_0_), channel_id=1, source_target_pairs={{0,64},{1,65},{2,66},{3,67},{4,68},{5,69},{6,70},{7,71},{8,72},{9,... | collective-permute-start | bytes 786440 | tf_op jit(solution)/shard_map/ppermute | solution.py:21
  11.9 7.6 %collective-permute-done.3.rest_4_ = bf16[8,128,128]{2,1,0:T(8,128)(2,1)S(1)} collective-permute-done((bf16[8,128,128]{2,1,0:T(8,128)(2,1)S(1)}, bf16[8,128,128]{2,1,0:T(8,128)(2,1)S(1)}, u32[]{:S(2)}, u32[]{:S(2)}) %collective-permute-start.3) | collective-permute-done | bytes 262176 | tf_op jit(solution)/shard_map/ppermute | solution.py:21
  19.5 2.8 %collective-permute-start.6 = (bf16[8,128,128]{2,1,0:T(8,128)(2,1)S(1)}, bf16[8,128,128]{2,1,0:T(8,128)(2,1)S(1)}, u32[]{:S(2)}, u32[]{:S(2)}) collective-permute-start(bf16[8,128,128]{2,1,0:T(8,128)(2,1)S(1)} %collective-permute-done.3.rest_4_), channel_id=1, source_target_pairs={{0,192},{1,193},{2,194},{3,195},{4,196},{5,197},{6,198},{7,199},{8... | collective-permute-start | bytes 786440 | tf_op jit(solution)/shard_map/ppermute | solution.py:21
  22.2 0.8 %collective-permute-start.5 = (bf16[8,128,128]{2,1,0:T(8,128)(2,1)S(1)}, bf16[8,128,128]{2,1,0:T(8,128)(2,1)S(1)}, u32[]{:S(2)}, u32[]{:S(2)}) collective-permute-start(bf16[8,128,128]{2,1,0:T(8,128)(2,1)S(1)} %collective-permute-done.3.rest_4_), channel_id=1, source_target_pairs={{0,128},{1,129},{2,130},{3,131},{4,132},{5,133},{6,134},{7,135},{8... | collective-permute-start | bytes 786440 | tf_op jit(solution)/shard_map/ppermute | solution.py:21
  23.0 0.0 collective-permute-done.2.rest_3_
  23.0 0.9 %collective-permute-start.4 = (bf16[8,128,128]{2,1,0:T(8,128)(2,1)S(1)}, bf16[8,128,128]{2,1,0:T(8,128)(2,1)S(1)}, u32[]{:S(2)}, u32[]{:S(2)}) collective-permute-start(bf16[8,128,128]{2,1,0:T(8,128)(2,1)S(1)} %collective-permute-done.3.rest_4_), channel_id=1, source_target_pairs={{0,64},{1,65},{2,66},{3,67},{4,68},{5,69},{6,70},{7,71},{8,72},{9,... | collective-permute-start | bytes 786440 | tf_op jit(solution)/shard_map/ppermute | solution.py:21
  23.9 0.0 collective-permute-done.1.rest_2_
  23.9 0.9 %collective-permute-done.rest_1_ = bf16[8,128,128]{2,1,0:T(8,128)(2,1)S(1)} collective-permute-done((bf16[8,128,128]{2,1,0:T(8,128)(2,1)S(1)}, bf16[8,128,128]{2,1,0:T(8,128)(2,1)S(1)}, u32[]{:S(2)}, u32[]{:S(2)}) %collective-permute-start) | collective-permute-done | bytes 262176 | tf_op jit(solution)/shard_map/ppermute | solution.py:21
  24.8 4.8 %collective-permute-start.8 = (bf16[1,128,128]{2,1,0:T(8,128)(2,1)S(1)}, bf16[1,128,128]{2,1,0:T(8,128)(2,1)S(1)}, u32[]{:S(2)}, u32[]{:S(2)}) collective-permute-start(bf16[1,128,128]{2,1,0:T(8,128)(2,1)S(1)} %fusion.1), channel_id=1, source_target_pairs={{0,31},{1,0},{2,1},{3,2},{4,3},{5,4},{6,5},{7,6},{8,7},{9,8},{10,9... | collective-permute-start | bytes 98312 | tf_op jit(solution)/shard_map/ppermute | solution.py:21
  29.6 2.4 %collective-permute-start.7 = (bf16[1,128,128]{2,1,0:T(8,128)(2,1)S(1)}, bf16[1,128,128]{2,1,0:T(8,128)(2,1)S(1)}, u32[]{:S(2)}, u32[]{:S(2)}) collective-permute-start(bf16[1,128,128]{2,1,0:T(8,128)(2,1)S(1)} %fusion.1), channel_id=1, source_target_pairs={{0,63},{1,32},{2,33},{3,34},{4,35},{5,36},{6,37},{7,38},{8,39},{9,... | collective-permute-start | bytes 98312 | tf_op jit(solution)/shard_map/ppermute | solution.py:21
  32.0 0.0 collective-permute-done.8
  32.0 6.4 %collective-permute-done.7 = bf16[1,128,128]{2,1,0:T(8,128)(2,1)S(1)} collective-permute-done((bf16[1,128,128]{2,1,0:T(8,128)(2,1)S(1)}, bf16[1,128,128]{2,1,0:T(8,128)(2,1)S(1)}, u32[]{:S(2)}, u32[]{:S(2)}) %collective-permute-start.7) | collective-permute-done | bytes 32800 | tf_op jit(solution)/shard_map/ppermute | solution.py:21
  38.4 0.0 collective-permute-done.6.rest_7_
  38.5 0.0 collective-permute-done.5.rest_6_
  38.5 0.0 collective-permute-done.4.rest_5_
  38.5 0.0 copy-start
  38.5 2.6 %copy-done = bf16[1,160,136,128]{3,2,1,0:T(8,128)(2,1)S(1)} copy-done((bf16[1,160,136,128]{3,2,1,0:T(8,128)(2,1)S(1)}, bf16[1,160,136,128]{3,2,1,0:T(8,128)(2,1)}, u32[]{:S(2)}) %copy-start) | copy-done | bytes 5570584
  41.1 0.0 copy-start.1
  41.1 0.7 %copy-done.1 = s32[160]{0:T(256)S(1)} copy-done((s32[160]{0:T(256)S(1)}, s32[160]{0:T(256)}, u32[]{:S(2)}) %copy-start.1) | copy-done | bytes 664
  41.7 0.0 copy-start.2
  41.7 0.7 %copy-done.2 = f32[160]{0:T(256)S(1)} copy-done((f32[160]{0:T(256)S(1)}, f32[160]{0:T(256)}, u32[]{:S(2)}) %copy-start.2) | copy-done | bytes 664
  42.4 6.6 %shard_map.46 = bf16[160,136,128]{2,1,0:T(8,128)(2,1)} custom-call(s32[1]{0:T(128)} %bitcast.me, s32[160]{0:T(256)S(1)} %copy-done.1, f32[160]{0:T(256)S(1)} %copy-done.2, bf16[160,136,128]{2,1,0:T(8,128)(2,1)S(1)} %bitcast.3, bf16[8,128,128]{2,1,0:T(8,128)(2,1)S(1)} %convert_element_type.3.rest_0_, bf16[8,128,128]{2,1,0:T(8,128)(2,1)S(1)} %collective-permute-done.rest_1_, ...), custom_call_target="tpu_custom_call" | custom-call | flops 1426063360 | bytes 11141120 | tf_op jit(solution)/shard_map/pallas_call | solution.py:78
  (2 shorter events, 0.0 us)
Async XLA Ops:
  1.1 18.4 %collective-permute-start.3 = (bf16[8,128,128]{2,1,0:T(8,128)(2,1)S(1)}, bf16[8,128,128]{2,1,0:T(8,128)(2,1)S(1)}, u32[]{:S(2)}, u32[]{:S(2)}) collective-permute-start(bf16[8,128,128]{2,1,0:T(8,128)(2,1)S(1)} %convert_element_type.3.rest_0_), channel_id=1, source_target_pairs={{0,32},{1,33},{2,34},{3,35},{4,36},{5,37},{6,38},{7,39},{8,40},{9,... | collective-permute-start | bytes 786440 | tf_op jit(solution)/shard_map/ppermute | solution.py:21
  7.5 15.6 %collective-permute-start.2 = (bf16[8,128,128]{2,1,0:T(8,128)(2,1)S(1)}, bf16[8,128,128]{2,1,0:T(8,128)(2,1)S(1)}, u32[]{:S(2)}, u32[]{:S(2)}) collective-permute-start(bf16[8,128,128]{2,1,0:T(8,128)(2,1)S(1)} %convert_element_type.3.rest_0_), channel_id=1, source_target_pairs={{0,192},{1,193},{2,194},{3,195},{4,196},{5,197},{6,198},{7,199},{8... | collective-permute-start | bytes 786440 | tf_op jit(solution)/shard_map/ppermute | solution.py:21
  10.2 13.7 %collective-permute-start.1 = (bf16[8,128,128]{2,1,0:T(8,128)(2,1)S(1)}, bf16[8,128,128]{2,1,0:T(8,128)(2,1)S(1)}, u32[]{:S(2)}, u32[]{:S(2)}) collective-permute-start(bf16[8,128,128]{2,1,0:T(8,128)(2,1)S(1)} %convert_element_type.3.rest_0_), channel_id=1, source_target_pairs={{0,128},{1,129},{2,130},{3,131},{4,132},{5,133},{6,134},{7,135},{8... | collective-permute-start | bytes 786440 | tf_op jit(solution)/shard_map/ppermute | solution.py:21
  11.0 13.8 %collective-permute-start = (bf16[8,128,128]{2,1,0:T(8,128)(2,1)S(1)}, bf16[8,128,128]{2,1,0:T(8,128)(2,1)S(1)}, u32[]{:S(2)}, u32[]{:S(2)}) collective-permute-start(bf16[8,128,128]{2,1,0:T(8,128)(2,1)S(1)} %convert_element_type.3.rest_0_), channel_id=1, source_target_pairs={{0,64},{1,65},{2,66},{3,67},{4,68},{5,69},{6,70},{7,71},{8,72},{9,... | collective-permute-start | bytes 786440 | tf_op jit(solution)/shard_map/ppermute | solution.py:21
  19.5 19.0 %collective-permute-start.6 = (bf16[8,128,128]{2,1,0:T(8,128)(2,1)S(1)}, bf16[8,128,128]{2,1,0:T(8,128)(2,1)S(1)}, u32[]{:S(2)}, u32[]{:S(2)}) collective-permute-start(bf16[8,128,128]{2,1,0:T(8,128)(2,1)S(1)} %collective-permute-done.3.rest_4_), channel_id=1, source_target_pairs={{0,192},{1,193},{2,194},{3,195},{4,196},{5,197},{6,198},{7,199},{8... | collective-permute-start | bytes 786440 | tf_op jit(solution)/shard_map/ppermute | solution.py:21
  22.2 16.2 %collective-permute-start.5 = (bf16[8,128,128]{2,1,0:T(8,128)(2,1)S(1)}, bf16[8,128,128]{2,1,0:T(8,128)(2,1)S(1)}, u32[]{:S(2)}, u32[]{:S(2)}) collective-permute-start(bf16[8,128,128]{2,1,0:T(8,128)(2,1)S(1)} %collective-permute-done.3.rest_4_), channel_id=1, source_target_pairs={{0,128},{1,129},{2,130},{3,131},{4,132},{5,133},{6,134},{7,135},{8... | collective-permute-start | bytes 786440 | tf_op jit(solution)/shard_map/ppermute | solution.py:21
  23.0 15.4 %collective-permute-start.4 = (bf16[8,128,128]{2,1,0:T(8,128)(2,1)S(1)}, bf16[8,128,128]{2,1,0:T(8,128)(2,1)S(1)}, u32[]{:S(2)}, u32[]{:S(2)}) collective-permute-start(bf16[8,128,128]{2,1,0:T(8,128)(2,1)S(1)} %collective-permute-done.3.rest_4_), channel_id=1, source_target_pairs={{0,64},{1,65},{2,66},{3,67},{4,68},{5,69},{6,70},{7,71},{8,72},{9,... | collective-permute-start | bytes 786440 | tf_op jit(solution)/shard_map/ppermute | solution.py:21
  24.8 7.1 %collective-permute-start.8 = (bf16[1,128,128]{2,1,0:T(8,128)(2,1)S(1)}, bf16[1,128,128]{2,1,0:T(8,128)(2,1)S(1)}, u32[]{:S(2)}, u32[]{:S(2)}) collective-permute-start(bf16[1,128,128]{2,1,0:T(8,128)(2,1)S(1)} %fusion.1), channel_id=1, source_target_pairs={{0,31},{1,0},{2,1},{3,2},{4,3},{5,4},{6,5},{7,6},{8,7},{9,8},{10,9... | collective-permute-start | bytes 98312 | tf_op jit(solution)/shard_map/ppermute | solution.py:21
  29.6 8.8 %collective-permute-start.7 = (bf16[1,128,128]{2,1,0:T(8,128)(2,1)S(1)}, bf16[1,128,128]{2,1,0:T(8,128)(2,1)S(1)}, u32[]{:S(2)}, u32[]{:S(2)}) collective-permute-start(bf16[1,128,128]{2,1,0:T(8,128)(2,1)S(1)} %fusion.1), channel_id=1, source_target_pairs={{0,63},{1,32},{2,33},{3,34},{4,35},{5,36},{6,37},{7,38},{8,39},{9,... | collective-permute-start | bytes 98312 | tf_op jit(solution)/shard_map/ppermute | solution.py:21
  38.5 2.6 %copy-start = (bf16[1,160,136,128]{3,2,1,0:T(8,128)(2,1)S(1)}, bf16[1,160,136,128]{3,2,1,0:T(8,128)(2,1)}, u32[]{:S(2)}) copy-start(bf16[1,160,136,128]{3,2,1,0:T(8,128)(2,1)} %param.4) | copy-start | bytes 16711684
  41.1 0.7 %copy-start.1 = (s32[160]{0:T(256)S(1)}, s32[160]{0:T(256)}, u32[]{:S(2)}) copy-start(s32[160]{0:T(256)} %cell.1) | copy-start | bytes 1924
  41.7 0.7 %copy-start.2 = (f32[160]{0:T(256)S(1)}, f32[160]{0:T(256)}, u32[]{:S(2)}) copy-start(f32[160]{0:T(256)} %fraction.1) | copy-start | bytes 1924
